TPU v7x, 32 devices: a whole 2x2x4 slice. The times are simulated.
32 devices in a mesh: ax: 2 (over x), az: 4 (over z), rad: 4 (over y, core).
Axes of the slice: x: 2, y: 2, z: 4, core: 2. Of those that a mesh axis runs over, the one named last changes fastest.
Arguments:
- velocity: float32 [512, 64, 512], P('rad', 'az', 'ax'), may hold values from -4 to 4
- radial_courant: bfloat16 [512, 64, 512], P('rad', 'az', 'ax'), may hold values from -0.5 to 0.5
- axial_courant: bfloat16 [512, 64, 512], P('rad', 'az', 'ax'), may hold values from -0.5 to 0.5
- radial_diffusion: float32 [512], P('rad'), may hold values from 2048 to 8192
Outputs:
- advanced: float32 [512, 64, 512], P('rad', 'az', 'ax')
All inputs are finite; a program needn't handle non-finite values.
Results may differ from a plain program's by a relative error of at most 0.0009.
Values sent between devices are 32-bit elements; how exact they have to be, the bound alone decides.
A program may use at most 64 MiB of HBM per device.

v0:
```python
from functools import partial
import jax
import jax.numpy as jnp
from jax import lax
from jax.sharding import PartitionSpec as P

NR = 512
STEPS = 6
theta_rate = 0.25
axial_mixing = 0.25
azimuth_mixing = 0.25


def padded(block, sides, width, periodic):
    for axis, dim in sides:
        count = lax.axis_size(axis)
        forward = [(i, i + 1) for i in range(count - 1)]
        if periodic:
            forward.append((count - 1, 0))
        backward = [(target, source) for source, target in forward]
        low = lax.ppermute(
            lax.slice_in_dim(block, block.shape[dim] - width, None, axis=dim), axis, forward
        )
        high = lax.ppermute(lax.slice_in_dim(block, 0, width, axis=dim), axis, backward)
        block = jnp.concatenate([low, block, high], axis=dim)
    return block


def radial_terms(radial_diffusion, position):
    spacing = 1.0 / (NR + 1)
    radius = 1.0 + (position + 1.0) * spacing
    inward = radial_diffusion * (radius - 0.5 * spacing) / radius
    outward = radial_diffusion * (radius + 0.5 * spacing) / radius
    curvature = radial_diffusion * spacing * spacing / (radius * radius)
    return (radius, inward, outward, curvature)


def right_side(
    state_field,
    radial_lower,
    radial_upper,
    axial_minus_two,
    axial_minus_one,
    axial_plus_one,
    axial_plus_two,
    azimuth_minus_two,
    azimuth_minus_one,
    azimuth_plus_one,
    azimuth_plus_two,
    radial_courant,
    axial_courant,
    radius,
    inward,
    outward,
    curvature,
):
    radius_col = radius[:, None, None]
    spread = (
        outward[:, None, None] * (radial_upper - state_field)
        - inward[:, None, None] * (state_field - radial_lower)
        - curvature[:, None, None] * state_field
    )
    radial_slope = 0.5 * (radial_upper - radial_lower)
    axial_slope = (
        8.0 * (axial_plus_one - axial_minus_one) - (axial_plus_two - axial_minus_two)
    ) / 12.0
    axial_curve = (
        16.0 * (axial_plus_one + axial_minus_one)
        - (axial_plus_two + axial_minus_two)
        - 30.0 * state_field
    ) / 12.0
    azimuth_slope = (
        8.0 * (azimuth_plus_one - azimuth_minus_one) - (azimuth_plus_two - azimuth_minus_two)
    ) / 12.0
    azimuth_curve = (
        16.0 * (azimuth_plus_one + azimuth_minus_one)
        - (azimuth_plus_two + azimuth_minus_two)
        - 30.0 * state_field
    ) / 12.0
    transport = (
        radial_courant * radial_slope
        + axial_courant * axial_slope
        + theta_rate * state_field * azimuth_slope / radius_col
    )
    mixing = axial_mixing * axial_curve + azimuth_mixing * azimuth_curve / (radius_col * radius_col)
    return state_field + spread - transport + mixing


def neighbours(state_field):
    slab_rows, theta_cells, axial_cells = state_field.shape
    radial_ext = padded(state_field, (("rad", 0),), 1, False)
    radial_lower = radial_ext[:-2]
    radial_upper = radial_ext[2:]
    azimuth_ext = padded(state_field, (("az", 1),), 2, True)
    axial_ext = padded(state_field, (("ax", 2),), 2, False)
    return (
        radial_lower,
        radial_upper,
        axial_ext[:, :, 0:axial_cells],
        axial_ext[:, :, 1 : axial_cells + 1],
        axial_ext[:, :, 3 : axial_cells + 3],
        axial_ext[:, :, 4 : axial_cells + 4],
        azimuth_ext[:, 0:theta_cells],
        azimuth_ext[:, 1 : theta_cells + 1],
        azimuth_ext[:, 3 : theta_cells + 3],
        azimuth_ext[:, 4 : theta_cells + 4],
    )


def join_slabs(earlier, later_seg):
    head_left, tail_left, tips_left = earlier
    head_right, tail_right, tips_right = later_seg
    divisor = 1.0 - tips_left[3] * tips_right[0]
    mid_value = (tail_left - tips_left[3] * head_right) / divisor
    mid_left = tips_left[2] / divisor
    mid_right = -tips_left[3] * tips_right[1] / divisor
    next_value = head_right - tips_right[0] * mid_value
    next_left = -tips_right[0] * mid_left
    next_right = tips_right[1] - tips_right[0] * mid_right
    new_head = head_left - tips_left[1] * next_value
    new_tail = tail_right - tips_right[2] * mid_value
    new_tips = jnp.stack(
        [
            tips_left[0] - tips_left[1] * next_left,
            -tips_left[1] * next_right,
            -tips_right[2] * mid_left,
            tips_right[3] - tips_right[2] * mid_right,
        ]
    )
    return (new_head, new_tail, new_tips)


def choose(keep_new, fresh_value, stale_value):
    return jnp.where(keep_new, fresh_value, stale_value)


def settle(prefix, own_slab, suffix):
    combined = join_slabs(own_slab, suffix)
    pre_first, pre_last, pre_tips = prefix
    own_first, own_last, own_tips = own_slab
    suf_first, suf_last, suf_tips = suffix
    lower_value = (pre_last - pre_tips[3] * combined[0]) / (1.0 - pre_tips[3] * combined[2][0])
    upper_value = (suf_first - suf_tips[0] * (own_last - own_tips[2] * lower_value)) / (
        1.0 - suf_tips[0] * own_tips[3]
    )
    return (lower_value, upper_value)


def interface(first_row, last_row, spike_tips, every_tips):
    own_slab = (first_row, last_row, spike_tips)
    identity = (
        jnp.zeros_like(first_row),
        jnp.zeros_like(last_row),
        jnp.array([0.0, -1.0, -1.0, 0.0], jnp.float32),
    )
    every_first, every_last = (
        lax.all_gather(first_row[None], "rad", axis=0, tiled=True),
        lax.all_gather(last_row[None], "rad", axis=0, tiled=True),
    )
    position = lax.axis_index("rad")
    slab_count = lax.axis_size("rad")
    prefix = identity
    for index_k in range(slab_count):
        member = (every_first[index_k], every_last[index_k], every_tips[index_k])
        joined = join_slabs(prefix, member)
        prefix = jax.tree.map(partial(choose, index_k < position), joined, prefix)
    suffix = identity
    for index_k in range(slab_count - 1, -1, -1):
        member = (every_first[index_k], every_last[index_k], every_tips[index_k])
        joined = join_slabs(member, suffix)
        suffix = jax.tree.map(partial(choose, index_k > position), joined, suffix)
    return settle(prefix, own_slab, suffix)


def local(velocity, radial_courant, axial_courant, radial_diffusion):
    slab_rows = velocity.shape[0]
    start_row = (lax.axis_index("rad") * slab_rows).astype(jnp.float32)
    position = start_row + jnp.arange(slab_rows).astype(jnp.float32)
    radius, inward, outward, curvature = radial_terms(radial_diffusion, position)
    zero_one = jnp.zeros((1,), jnp.float32)
    lower_diag = jnp.concatenate([zero_one, -inward[1:]])
    upper_diag = jnp.concatenate([-outward[:-1], zero_one])
    main_diag = 1.0 + inward + outward + curvature
    inverse = lax.linalg.tridiagonal_solve(
        lower_diag, main_diag, upper_diag, jnp.eye(slab_rows, dtype=jnp.float32)
    )
    left_spike = -inward[0] * inverse[:, 0]
    right_spike = -outward[-1] * inverse[:, -1]
    spike_tips = jnp.stack([left_spike[0], right_spike[0], left_spike[-1], right_spike[-1]])
    every_tips = lax.all_gather(spike_tips[None], "rad", axis=0, tiled=True)
    state_field = velocity
    for turn_index in range(STEPS):
        right_hand = right_side(
            state_field,
            *neighbours(state_field),
            radial_courant,
            axial_courant,
            radius,
            inward,
            outward,
            curvature
        )
        flat_rhs = right_hand.reshape(slab_rows, -1)
        slab_solution = jnp.dot(
            inverse, flat_rhs, precision=lax.Precision.HIGHEST, preferred_element_type=jnp.float32
        )
        lower_value, upper_value = interface(
            slab_solution[0], slab_solution[-1], spike_tips, every_tips
        )
        solved = (
            slab_solution
            - left_spike[:, None] * lower_value[None, :]
            - right_spike[:, None] * upper_value[None, :]
        )
        state_field = solved.reshape(state_field.shape)
    return state_field


def solution(mesh):
    return jax.shard_map(
        local,
        mesh=mesh,
        in_specs=(P("rad", "az", "ax"), P("rad", "az", "ax"), P("rad", "az", "ax"), P("rad")),
        out_specs=P("rad", "az", "ax"),
        check_vma=False,
    )
```

profile of v0, /device:TPU:0, one launch (start us, length us, event | category | flops | bytes accessed | tf_op | source)
XLA Modules:
  0.0 981.2 jit_solution(10601417094346248530)
XLA Ops:
  26.0 253.8 %while.32 = (s32[]{:T(128)}, f32[]{:T(128)}, f32[128]{0:T(128)S(1)}, f32[3,32]{1,0:T(4,128)S(1)}, f32[3,32,128]{2,1,0:T(8,128)S(1)}, /*index=5*/f32[3,32]{1,0:T(...) while((s32[]{:T(128)}, f32[]{:T(128)}, ...), condition=%wide.region_1.2_spmd, body=%wide.region_0.1_spmd.sunk | while | flops 12417 | bytes 104185 | solution.py:184
  90.2 20.2 %fusion.565 = (f32[128]{0:T(128)S(1)}, f32[128]{0:T(128)S(1)}, f32[128]{0:T(128)S(1)}, f32[128]{0:T(128)S(1)}, f32[128]{0:T(128)S(1)}, /*index=5*/f32[128]{0:T(1...) fusion(f32[3,32,128]{2,1,0:T(8,128)S(1)} %get-tuple-element.125, ...), kind=kLoop, calls=%fused_computation.41.clone.1 | loop fusion | flops 12288 | bytes 33664 | tf_op jit(solution)/shard_map/while/body/eval_jaxpr/div | solution.py:184
  174.8 20.2 %fusion.565 = (f32[128]{0:T(128)S(1)}, f32[128]{0:T(128)S(1)}, f32[128]{0:T(128)S(1)}, f32[128]{0:T(128)S(1)}, f32[128]{0:T(128)S(1)}, /*index=5*/f32[128]{0:T(1...) fusion(f32[3,32,128]{2,1,0:T(8,128)S(1)} %get-tuple-element.125, ...), kind=kLoop, calls=%fused_computation.41.clone.1 | loop fusion | flops 12288 | bytes 33664 | tf_op jit(solution)/shard_map/while/body/eval_jaxpr/div | solution.py:184
  259.4 20.2 %fusion.565 = (f32[128]{0:T(128)S(1)}, f32[128]{0:T(128)S(1)}, f32[128]{0:T(128)S(1)}, f32[128]{0:T(128)S(1)}, f32[128]{0:T(128)S(1)}, /*index=5*/f32[128]{0:T(1...) fusion(f32[3,32,128]{2,1,0:T(8,128)S(1)} %get-tuple-element.125, ...), kind=kLoop, calls=%fused_computation.41.clone.1 | loop fusion | flops 12288 | bytes 33664 | tf_op jit(solution)/shard_map/while/body/eval_jaxpr/div | solution.py:184
  342.2 19.2 %fusion.330 = (f32[128]{0:T(128)S(1)}, f32[128]{0:T(128)S(1)}, f32[128]{0:T(128)S(1)}, f32[128]{0:T(128)S(1)}, f32[128]{0:T(128)S(1)}, /*index=5*/f32[128]{0:T(1...) fusion(f32[128,128]{1,0:T(8,128)S(1)} %fusion.256, ...), kind=kLoop, calls=%fused_computation.662 | loop fusion | flops 11904 | bytes 32504 | tf_op jit(solution)/shard_map/eval_jaxpr/div | solution.py:184
  361.8 65.2 %while.33 = (s32[]{:T(128)}, f32[128]{0:T(128)S(1)}, f32[3,32,128]{2,1,0:T(8,128)S(1)}, f32[3,32,128]{2,1,0:T(8,128)S(1)}, f32[3,32]{1,0:T(4,128)S(1)}, /*index=...) while((s32[]{:T(128)}, f32[128]{0:T(128)S(1)}, ...), condition=%wide.region_3.4_spmd, body=%wide.region_2.3_spmd.sunk | while | flops 8226 | bytes 101341 | solution.py:184
  363.3 20.2 %fusion.568 = (f32[128]{0:T(128)S(1)}, f32[128]{0:T(128)S(1)}, f32[128]{0:T(128)S(1)}, f32[128]{0:T(128)S(1)}, f32[128]{0:T(128)S(1)}, /*index=5*/f32[128]{0:T(1...) fusion(f32[3,32,128]{2,1,0:T(8,128)S(1)} %get-tuple-element.136, ...), kind=kLoop, calls=%fused_computation.169.clone.1 | loop fusion | flops 8192 | bytes 33536 | tf_op jit(solution)/shard_map/while/body/eval_jaxpr/sub | solution.py:184
  385.0 20.2 %fusion.568 = (f32[128]{0:T(128)S(1)}, f32[128]{0:T(128)S(1)}, f32[128]{0:T(128)S(1)}, f32[128]{0:T(128)S(1)}, f32[128]{0:T(128)S(1)}, /*index=5*/f32[128]{0:T(1...) fusion(f32[3,32,128]{2,1,0:T(8,128)S(1)} %get-tuple-element.136, ...), kind=kLoop, calls=%fused_computation.169.clone.1 | loop fusion | flops 8192 | bytes 33536 | tf_op jit(solution)/shard_map/while/body/eval_jaxpr/sub | solution.py:184
  406.8 20.2 %fusion.568 = (f32[128]{0:T(128)S(1)}, f32[128]{0:T(128)S(1)}, f32[128]{0:T(128)S(1)}, f32[128]{0:T(128)S(1)}, f32[128]{0:T(128)S(1)}, /*index=5*/f32[128]{0:T(1...) fusion(f32[3,32,128]{2,1,0:T(8,128)S(1)} %get-tuple-element.136, ...), kind=kLoop, calls=%fused_computation.169.clone.1 | loop fusion | flops 8192 | bytes 33536 | tf_op jit(solution)/shard_map/while/body/eval_jaxpr/sub | solution.py:184
  580.3 14.9 %fusion.181 = f32[128,16,256]{2,1,0:T(8,128)S(1)} fusion(bf16[128,16,256]{2,1,0:T(8,128)(2,1)S(1)} %copy-done, bf16[128,16,256]{2,1,0:T(8,128)(2,1)S(1)} %copy-done.1, f32[128,16,256]{2,1,0:T(8,128)} %param.14, f32[1,16,256]{2,1,0:T(8,128)} %collective-permute-done.1, f32[1,16,256]{2,1,0:T(8,128)S(1)} %collective-permute-done, ...), kind=kLoop, calls=%fused_computation.299 | loop fusion | flops 28311552 | bytes 10816000 | tf_op jit(solution)/shard_map/add | solution.py:86
  610.0 13.5 %subtract_divide_fusion.5 = (f32[1,4096]{1,0:T(1,128)S(1)}, f32[1,4096]{1,0:T(1,128)S(1)}) fusion(f32[]{:T(128)} %bitcast.672, f32[]{:T(128)S(6)} %sub.2725, f32[]{:T(128)S(1)} %bitcast.2392, f32[128,4096]{1,0:T(8,128)S(1)} %fusion.531, f32[]{:T(128)S(6)} %sub.2730, f32[]{:T(128)} %bitcast.670, f32[]{:T(128)} %bitcast.640, f32[]{:T(128)} %bitcast.639, ...), kind=kLoop, calls=%fused_computation.547 | loop fusion | flops 286720 | bytes 196748 | tf_op jit(solution)/shard_map/div | solution.py:143
  654.5 9.4 fusion.185
  680.9 13.5 %subtract_divide_fusion.4 = (f32[1,4096]{1,0:T(1,128)S(1)}, f32[1,4096]{1,0:T(1,128)S(1)}) fusion(f32[]{:T(128)} %bitcast.672, f32[]{:T(128)S(6)} %sub.2725, f32[]{:T(128)S(1)} %bitcast.2393, f32[128,4096]{1,0:T(8,128)S(1)} %fusion.532, f32[]{:T(128)S(6)} %sub.2730, f32[]{:T(128)} %bitcast.670, f32[]{:T(128)} %bitcast.640, f32[]{:T(128)} %bitcast.639, ...), kind=kLoop, calls=%fused_computation.546 | loop fusion | flops 286720 | bytes 196748 | tf_op jit(solution)/shard_map/div | solution.py:143
  725.3 9.4 fusion.189
  738.4 7.9 all-gather.6
  751.9 13.5 %subtract_divide_fusion.3 = (f32[1,4096]{1,0:T(1,128)S(1)}, f32[1,4096]{1,0:T(1,128)S(1)}) fusion(f32[]{:T(128)} %bitcast.672, f32[]{:T(128)S(6)} %sub.2725, f32[]{:T(128)S(1)} %bitcast.2394, f32[128,4096]{1,0:T(8,128)S(1)} %fusion.533, f32[]{:T(128)S(6)} %sub.2730, f32[]{:T(128)} %bitcast.670, f32[]{:T(128)} %bitcast.640, f32[]{:T(128)} %bitcast.639, ...), kind=kLoop, calls=%fused_computation.545 | loop fusion | flops 286720 | bytes 196748 | tf_op jit(solution)/shard_map/div | solution.py:143
  796.6 9.4 fusion.193
  809.6 7.9 all-gather.8
  823.1 13.5 %subtract_divide_fusion.2 = (f32[1,4096]{1,0:T(1,128)S(1)}, f32[1,4096]{1,0:T(1,128)S(1)}) fusion(f32[]{:T(128)} %bitcast.672, f32[]{:T(128)S(6)} %sub.2725, f32[]{:T(128)S(1)} %bitcast.2395, f32[128,4096]{1,0:T(8,128)S(1)} %fusion.534, f32[]{:T(128)S(6)} %sub.2730, f32[]{:T(128)} %bitcast.670, f32[]{:T(128)} %bitcast.640, f32[]{:T(128)} %bitcast.639, ...), kind=kLoop, calls=%fused_computation.544 | loop fusion | flops 286720 | bytes 196748 | tf_op jit(solution)/shard_map/div | solution.py:143
  867.5 9.4 fusion.197
  894.1 13.5 %subtract_divide_fusion.1 = (f32[1,4096]{1,0:T(1,128)S(1)}, f32[1,4096]{1,0:T(1,128)S(1)}) fusion(f32[]{:T(128)} %bitcast.672, f32[]{:T(128)S(6)} %sub.2725, f32[]{:T(128)S(1)} %bitcast.2396, f32[128,4096]{1,0:T(8,128)S(1)} %fusion.535, f32[]{:T(128)S(6)} %sub.2730, f32[]{:T(128)} %bitcast.670, f32[]{:T(128)} %bitcast.640, f32[]{:T(128)} %bitcast.639, ...), kind=kLoop, calls=%fused_computation.543 | loop fusion | flops 286720 | bytes 196748 | tf_op jit(solution)/shard_map/div | solution.py:143
  938.6 9.4 fusion.201
  951.6 7.9 all-gather.12
  965.1 13.5 %subtract_divide_fusion = (f32[1,4096]{1,0:T(1,128)S(1)}, f32[1,4096]{1,0:T(1,128)S(1)}) fusion(f32[]{:T(128)} %bitcast.672, f32[]{:T(128)S(6)} %sub.2725, f32[]{:T(128)S(1)} %bitcast.2397, f32[128,4096]{1,0:T(8,128)S(1)} %fusion.536, f32[]{:T(128)S(6)} %sub.2730, f32[]{:T(128)} %bitcast.670, f32[]{:T(128)} %bitcast.640, f32[]{:T(128)} %bitcast.639, ...), kind=kLoop, calls=%fused_computation.542 | loop fusion | flops 286720 | bytes 196748 | tf_op jit(solution)/shard_map/div | solution.py:143
  (357 shorter events, 368.9 us)
Async XLA Ops:
  1.3 579.0 %collective-permute-start.1 = (f32[1,16,256]{2,1,0:T(8,128)}, f32[1,16,256]{2,1,0:T(8,128)}, u32[]{:S(2)}, u32[]{:S(2)}) collective-permute-start(f32[1,16,256]{2,1,0:T(8,128)} %get-tuple-element.511), channel_id=1, source_target_pairs={{0,1},{1,2},{2,3},{4,5},{5,6},{6,7},{8,9},{9,10},{10,11},{12,13},{... | collective-permute-start | bytes 49160 | tf_op jit(solution)/shard_map/ppermute | solution.py:21
  6.8 573.5 %collective-permute-start.5 = (f32[128,2,256]{2,1,0:T(2,128)}, f32[128,2,256]{2,1,0:T(2,128)S(1)}, u32[]{:S(2)}, u32[]{:S(2)}) collective-permute-start(f32[128,2,256]{2,1,0:T(2,128)} %get-tuple-element.509), channel_id=1, source_target_pairs={{0,4},{4,8},{8,12},{12,0},{1,5},{5,9},{9,13},{13,1},{2,6},{6,10},{... | collective-permute-start | bytes 786440 | tf_op jit(solution)/shard_map/ppermute | solution.py:21
  9.2 569.3 %collective-permute-start.4 = (f32[128,2,256]{2,1,0:T(2,128)}, f32[128,2,256]{2,1,0:T(2,128)}, u32[]{:S(2)}, u32[]{:S(2)}) collective-permute-start(f32[128,2,256]{2,1,0:T(2,128)} %get-tuple-element.508), channel_id=1, source_target_pairs={{4,0},{8,4},{12,8},{0,12},{5,1},{9,5},{13,9},{1,13},{6,2},{10,6},{... | collective-permute-start | bytes 786440 | tf_op jit(solution)/shard_map/ppermute | solution.py:24
  14.2 559.2 %collective-permute-start.2 = (f32[128,16,2]{0,1,2:T(8,128)}, f32[128,16,2]{0,1,2:T(8,128)}, u32[]{:S(2)}, u32[]{:S(2)}) collective-permute-start(f32[128,16,2]{0,1,2:T(8,128)} %copy.101), channel_id=1, source_target_pairs={{16,0},{17,1},{18,2},{19,3},{20,4},{21,5},{22,6},{23,7},{24,8},{25... | collective-permute-start | bytes 49160 | tf_op jit(solution)/shard_map/ppermute | solution.py:24
  16.5 559.9 %collective-permute-start.3 = (f32[128,16,2]{0,1,2:T(8,128)}, f32[128,16,2]{0,1,2:T(8,128)}, u32[]{:S(2)}, u32[]{:S(2)}) collective-permute-start(f32[128,16,2]{0,1,2:T(8,128)} %copy.102), channel_id=1, source_target_pairs={{0,16},{1,17},{2,18},{3,19},{4,20},{5,21},{6,22},{7,23},{8,24},{9,... | collective-permute-start | bytes 49160 | tf_op jit(solution)/shard_map/ppermute | solution.py:21
  627.9 26.6 %collective-permute-start.11 = (f32[128,2,256]{2,1,0:T(2,128)}, f32[128,2,256]{2,1,0:T(2,128)S(1)}, u32[]{:S(2)}, u32[]{:S(2)}) collective-permute-start(f32[128,2,256]{2,1,0:T(2,128)} %get-tuple-element.503), channel_id=1, source_target_pairs={{0,4},{4,8},{8,12},{12,0},{1,5},{5,9},{9,13},{13,1},{2,6},{6,10},{... | collective-permute-start | bytes 786440 | tf_op jit(solution)/shard_map/ppermute | solution.py:21
  627.9 24.8 %collective-permute-start.10 = (f32[128,2,256]{2,1,0:T(2,128)}, f32[128,2,256]{2,1,0:T(2,128)}, u32[]{:S(2)}, u32[]{:S(2)}) collective-permute-start(f32[128,2,256]{2,1,0:T(2,128)} %get-tuple-element.502), channel_id=1, source_target_pairs={{4,0},{8,4},{12,8},{0,12},{5,1},{9,5},{13,9},{1,13},{6,2},{10,6},{... | collective-permute-start | bytes 786440 | tf_op jit(solution)/shard_map/ppermute | solution.py:24
  635.4 12.2 %collective-permute-start.8 = (f32[128,16,2]{0,1,2:T(8,128)}, f32[128,16,2]{0,1,2:T(8,128)S(1)}, u32[]{:S(2)}, u32[]{:S(2)}) collective-permute-start(f32[128,16,2]{0,1,2:T(8,128)} %copy.103), channel_id=1, source_target_pairs={{16,0},{17,1},{18,2},{19,3},{20,4},{21,5},{22,6},{23,7},{24,8},{25... | collective-permute-start | bytes 49160 | tf_op jit(solution)/shard_map/ppermute | solution.py:24
  639.0 11.6 %collective-permute-start.9 = (f32[128,16,2]{0,1,2:T(8,128)}, f32[128,16,2]{0,1,2:T(8,128)}, u32[]{:S(2)}, u32[]{:S(2)}) collective-permute-start(f32[128,16,2]{0,1,2:T(8,128)} %copy.104), channel_id=1, source_target_pairs={{0,16},{1,17},{2,18},{3,19},{4,20},{5,21},{6,22},{7,23},{8,24},{9,... | collective-permute-start | bytes 49160 | tf_op jit(solution)/shard_map/ppermute | solution.py:21
  698.7 26.7 %collective-permute-start.17 = (f32[128,2,256]{2,1,0:T(2,128)}, f32[128,2,256]{2,1,0:T(2,128)S(1)}, u32[]{:S(2)}, u32[]{:S(2)}) collective-permute-start(f32[128,2,256]{2,1,0:T(2,128)} %get-tuple-element.497), channel_id=1, source_target_pairs={{0,4},{4,8},{8,12},{12,0},{1,5},{5,9},{9,13},{13,1},{2,6},{6,10},{... | collective-permute-start | bytes 786440 | tf_op jit(solution)/shard_map/ppermute | solution.py:21
  698.7 24.9 %collective-permute-start.16 = (f32[128,2,256]{2,1,0:T(2,128)}, f32[128,2,256]{2,1,0:T(2,128)}, u32[]{:S(2)}, u32[]{:S(2)}) collective-permute-start(f32[128,2,256]{2,1,0:T(2,128)} %get-tuple-element.496), channel_id=1, source_target_pairs={{4,0},{8,4},{12,8},{0,12},{5,1},{9,5},{13,9},{1,13},{6,2},{10,6},{... | collective-permute-start | bytes 786440 | tf_op jit(solution)/shard_map/ppermute | solution.py:24
  706.3 12.2 %collective-permute-start.14 = (f32[128,16,2]{0,1,2:T(8,128)}, f32[128,16,2]{0,1,2:T(8,128)S(1)}, u32[]{:S(2)}, u32[]{:S(2)}) collective-permute-start(f32[128,16,2]{0,1,2:T(8,128)} %copy.105), channel_id=1, source_target_pairs={{16,0},{17,1},{18,2},{19,3},{20,4},{21,5},{22,6},{23,7},{24,8},{25... | collective-permute-start | bytes 49160 | tf_op jit(solution)/shard_map/ppermute | solution.py:24
  709.8 11.6 %collective-permute-start.15 = (f32[128,16,2]{0,1,2:T(8,128)}, f32[128,16,2]{0,1,2:T(8,128)}, u32[]{:S(2)}, u32[]{:S(2)}) collective-permute-start(f32[128,16,2]{0,1,2:T(8,128)} %copy.106), channel_id=1, source_target_pairs={{0,16},{1,17},{2,18},{3,19},{4,20},{5,21},{6,22},{7,23},{8,24},{9,... | collective-permute-start | bytes 49160 | tf_op jit(solution)/shard_map/ppermute | solution.py:21
  769.7 26.8 %collective-permute-start.23 = (f32[128,2,256]{2,1,0:T(2,128)}, f32[128,2,256]{2,1,0:T(2,128)S(1)}, u32[]{:S(2)}, u32[]{:S(2)}) collective-permute-start(f32[128,2,256]{2,1,0:T(2,128)} %get-tuple-element.491), channel_id=1, source_target_pairs={{0,4},{4,8},{8,12},{12,0},{1,5},{5,9},{9,13},{13,1},{2,6},{6,10},{... | collective-permute-start | bytes 786440 | tf_op jit(solution)/shard_map/ppermute | solution.py:21
  769.7 25.0 %collective-permute-start.22 = (f32[128,2,256]{2,1,0:T(2,128)}, f32[128,2,256]{2,1,0:T(2,128)}, u32[]{:S(2)}, u32[]{:S(2)}) collective-permute-start(f32[128,2,256]{2,1,0:T(2,128)} %get-tuple-element.490), channel_id=1, source_target_pairs={{4,0},{8,4},{12,8},{0,12},{5,1},{9,5},{13,9},{1,13},{6,2},{10,6},{... | collective-permute-start | bytes 786440 | tf_op jit(solution)/shard_map/ppermute | solution.py:24
  777.3 12.2 %collective-permute-start.20 = (f32[128,16,2]{0,1,2:T(8,128)}, f32[128,16,2]{0,1,2:T(8,128)S(1)}, u32[]{:S(2)}, u32[]{:S(2)}) collective-permute-start(f32[128,16,2]{0,1,2:T(8,128)} %copy.107), channel_id=1, source_target_pairs={{16,0},{17,1},{18,2},{19,3},{20,4},{21,5},{22,6},{23,7},{24,8},{25... | collective-permute-start | bytes 49160 | tf_op jit(solution)/shard_map/ppermute | solution.py:24
  780.8 11.8 %collective-permute-start.21 = (f32[128,16,2]{0,1,2:T(8,128)}, f32[128,16,2]{0,1,2:T(8,128)}, u32[]{:S(2)}, u32[]{:S(2)}) collective-permute-start(f32[128,16,2]{0,1,2:T(8,128)} %copy.108), channel_id=1, source_target_pairs={{0,16},{1,17},{2,18},{3,19},{4,20},{5,21},{6,22},{7,23},{8,24},{9,... | collective-permute-start | bytes 49160 | tf_op jit(solution)/shard_map/ppermute | solution.py:21
  840.9 26.6 %collective-permute-start.29 = (f32[128,2,256]{2,1,0:T(2,128)}, f32[128,2,256]{2,1,0:T(2,128)S(1)}, u32[]{:S(2)}, u32[]{:S(2)}) collective-permute-start(f32[128,2,256]{2,1,0:T(2,128)} %get-tuple-element.485), channel_id=1, source_target_pairs={{0,4},{4,8},{8,12},{12,0},{1,5},{5,9},{9,13},{13,1},{2,6},{6,10},{... | collective-permute-start | bytes 786440 | tf_op jit(solution)/shard_map/ppermute | solution.py:21
  840.9 24.8 %collective-permute-start.28 = (f32[128,2,256]{2,1,0:T(2,128)}, f32[128,2,256]{2,1,0:T(2,128)}, u32[]{:S(2)}, u32[]{:S(2)}) collective-permute-start(f32[128,2,256]{2,1,0:T(2,128)} %get-tuple-element.484), channel_id=1, source_target_pairs={{4,0},{8,4},{12,8},{0,12},{5,1},{9,5},{13,9},{1,13},{6,2},{10,6},{... | collective-permute-start | bytes 786440 | tf_op jit(solution)/shard_map/ppermute | solution.py:24
  848.5 12.2 %collective-permute-start.26 = (f32[128,16,2]{0,1,2:T(8,128)}, f32[128,16,2]{0,1,2:T(8,128)S(1)}, u32[]{:S(2)}, u32[]{:S(2)}) collective-permute-start(f32[128,16,2]{0,1,2:T(8,128)} %copy.109), channel_id=1, source_target_pairs={{16,0},{17,1},{18,2},{19,3},{20,4},{21,5},{22,6},{23,7},{24,8},{25... | collective-permute-start | bytes 49160 | tf_op jit(solution)/shard_map/ppermute | solution.py:24
  911.9 26.7 %collective-permute-start.35 = (f32[128,2,256]{2,1,0:T(2,128)}, f32[128,2,256]{2,1,0:T(2,128)S(1)}, u32[]{:S(2)}, u32[]{:S(2)}) collective-permute-start(f32[128,2,256]{2,1,0:T(2,128)} %get-tuple-element.479), channel_id=1, source_target_pairs={{0,4},{4,8},{8,12},{12,0},{1,5},{5,9},{9,13},{13,1},{2,6},{6,10},{... | collective-permute-start | bytes 786440 | tf_op jit(solution)/shard_map/ppermute | solution.py:21
  911.9 24.9 %collective-permute-start.34 = (f32[128,2,256]{2,1,0:T(2,128)}, f32[128,2,256]{2,1,0:T(2,128)}, u32[]{:S(2)}, u32[]{:S(2)}) collective-permute-start(f32[128,2,256]{2,1,0:T(2,128)} %get-tuple-element.478), channel_id=1, source_target_pairs={{4,0},{8,4},{12,8},{0,12},{5,1},{9,5},{13,9},{1,13},{6,2},{10,6},{... | collective-permute-start | bytes 786440 | tf_op jit(solution)/shard_map/ppermute | solution.py:24
  919.5 12.2 %collective-permute-start.32 = (f32[128,16,2]{0,1,2:T(8,128)}, f32[128,16,2]{0,1,2:T(8,128)S(1)}, u32[]{:S(2)}, u32[]{:S(2)}) collective-permute-start(f32[128,16,2]{0,1,2:T(8,128)} %copy.111), channel_id=1, source_target_pairs={{16,0},{17,1},{18,2},{19,3},{20,4},{21,5},{22,6},{23,7},{24,8},{25... | collective-permute-start | bytes 49160 | tf_op jit(solution)/shard_map/ppermute | solution.py:24
  923.0 11.6 %collective-permute-start.33 = (f32[128,16,2]{0,1,2:T(8,128)}, f32[128,16,2]{0,1,2:T(8,128)}, u32[]{:S(2)}, u32[]{:S(2)}) collective-permute-start(f32[128,16,2]{0,1,2:T(8,128)} %copy.112), channel_id=1, source_target_pairs={{0,16},{1,17},{2,18},{3,19},{4,20},{5,21},{6,22},{7,23},{8,24},{9,... | collective-permute-start | bytes 49160 | tf_op jit(solution)/shard_map/ppermute | solution.py:21
  (23 other events, 383.9 us)
where the time goes:
time: 998 us; the launch traced here: 981 us
  other arithmetic  333 us (33%)
  loops' own time  180 us (18%)
  local copies, waits for them, and re-layouts  166 us (17%)
  between operations  126 us (13%)
  blocking collectives  84.3 us (8%)
  starting transfers between devices  81.3 us (8%)
  matrix products  11.7 us (1%)
    another operation x2, loops' own time, local(): lax.linalg.tridiagonal_solve(lower_diag, main_diag, upper_diag, jnp.eye(s...  180 us
    div x6, other arithmetic, settle(): (suf_first - suf_tips[0] * (own_last - own_tips[2] * lower_value)) / (1.0...  80.8 us
    div x5, other arithmetic, local(): lax.linalg.tridiagonal_solve(lower_diag, main_diag, upper_diag, jnp.eye(s...  80.3 us
    add x6, other arithmetic, right_side(): return state_field + spread - transport + mixing  62.1 us
    sub x3, other arithmetic, local(): lax.linalg.tridiagonal_solve(lower_diag, main_diag, upper_diag, jnp.eye(s...  60.5 us
    unnamed x60, local copies, waits for them, and re-layouts  53.3 us
    all_gather x6, blocking collectives, interface(): lax.all_gather(first_row[None], 'rad', axis=0, tiled=True)  45.4 us
    ppermute x18, starting transfers between devices, padded(): lax.ppermute(lax.slice_in_dim(block, block.shape[dim] - width, None, axis...  43.1 us
  transfers between devices with their start and end apart: 36, of which 0 were waited for; matrix products, arithmetic and copies ran while one was open for 33% of the time, Pallas kernels for 0%

commit v1 on v0

--- a/solution.py
+++ b/solution.py
@@ -155,7 +155,9 @@
     )
     every_first, every_last = (
         lax.all_gather(first_row[None], "rad", axis=0, tiled=True),
-        lax.all_gather(last_row[None], "rad", axis=0, tiled=True),
+        jnp.concatenate(
+            lax.all_to_all(jnp.stack([last_row[None]] * lax.axis_size("rad")), "rad", 0, 0), axis=0
+        ),
     )
     position = lax.axis_index("rad")
     slab_count = lax.axis_size("rad")

time: 998 us -> 992 us (level)
  blocking collectives: 84.3 us -> 38.4 us
  starting transfers between devices: 81.3 us -> 115 us
    all_to_all x0 -> x6, starting transfers between devices: none -> 34.2 us  [interface(): lax.all_to_all(jnp.stack([last_row[None]] * lax.axis_size('rad')), 'rad',...]
    all_gather x6 -> x0, blocking collectives: 32.9 us -> none  [interface(): lax.all_gather(last_row[None], 'rad', axis=0, tiled=True)]
    all_gather x6, blocking collectives: 45.4 us -> 32.4 us  [interface(): lax.all_gather(first_row[None], 'rad', axis=0, tiled=True)]
  transfers between devices with their start and end apart: 36 -> 42, of which waited for: 0 -> 0; matrix products, arithmetic and copies ran while one was open for 33% -> 33% of each run, Pallas kernels for 0% -> 0%
where the time goes in v1:
time: 992 us; the launch traced here: 974 us
  other arithmetic  334 us (34%)
  loops' own time  179 us (18%)
  local copies, waits for them, and re-layouts  169 us (17%)
  between operations  126 us (13%)
  starting transfers between devices  115 us (12%)
  blocking collectives  38.4 us (4%)
  matrix products  11.6 us (1%)
    another operation x2, loops' own time, local(): lax.linalg.tridiagonal_solve(lower_diag, main_diag, upper_diag, jnp.eye(s...  179 us
    div x6, other arithmetic, settle(): (suf_first - suf_tips[0] * (own_last - own_tips[2] * lower_value)) / (1.0...  81.8 us
    div x5, other arithmetic, local(): lax.linalg.tridiagonal_solve(lower_diag, main_diag, upper_diag, jnp.eye(s...  79.8 us
    add x6, other arithmetic, right_side(): return state_field + spread - transport + mixing  62.8 us
    sub x3, other arithmetic, local(): lax.linalg.tridiagonal_solve(lower_diag, main_diag, upper_diag, jnp.eye(s...  61.3 us
    unnamed x60, local copies, waits for them, and re-layouts  53.2 us
    ppermute x18, starting transfers between devices, padded(): lax.ppermute(lax.slice_in_dim(block, block.shape[dim] - width, None, axis...  43.1 us
    broadcast_in_dim x17, other arithmetic, local(): lax.linalg.tridiagonal_solve(lower_diag, main_diag, upper_diag, jnp.eye(s...  42.5 us
  transfers between devices with their start and end apart: 42, of which 0 were waited for; matrix products, arithmetic and copies ran while one was open for 33% of the time, Pallas kernels for 0%

profile of v1, /device:TPU:0, one launch (start us, length us, event | category | flops | bytes accessed | tf_op | source)
XLA Modules:
  0.0 974.4 jit_solution(9999021812344193716)
XLA Ops:
  26.1 252.6 %while.32 = (s32[]{:T(128)}, f32[]{:T(128)}, f32[128]{0:T(128)S(1)}, f32[3,32]{1,0:T(4,128)S(1)}, f32[3,32,128]{2,1,0:T(8,128)S(1)}, /*index=5*/f32[3,32]{1,0:T(...) while((s32[]{:T(128)}, f32[]{:T(128)}, ...), condition=%wide.region_1.2_spmd, body=%wide.region_0.1_spmd.sunk | while | flops 12417 | bytes 104185 | solution.py:186
  90.1 19.9 %fusion.565 = (f32[128]{0:T(128)S(1)}, f32[128]{0:T(128)S(1)}, f32[128]{0:T(128)S(1)}, f32[128]{0:T(128)S(1)}, f32[128]{0:T(128)S(1)}, /*index=5*/f32[128]{0:T(1...) fusion(f32[3,32,128]{2,1,0:T(8,128)S(1)} %get-tuple-element.125, ...), kind=kLoop, calls=%fused_computation.41.clone.1 | loop fusion | flops 12288 | bytes 33664 | tf_op jit(solution)/shard_map/while/body/eval_jaxpr/div | solution.py:186
  174.3 19.9 %fusion.565 = (f32[128]{0:T(128)S(1)}, f32[128]{0:T(128)S(1)}, f32[128]{0:T(128)S(1)}, f32[128]{0:T(128)S(1)}, f32[128]{0:T(128)S(1)}, /*index=5*/f32[128]{0:T(1...) fusion(f32[3,32,128]{2,1,0:T(8,128)S(1)} %get-tuple-element.125, ...), kind=kLoop, calls=%fused_computation.41.clone.1 | loop fusion | flops 12288 | bytes 33664 | tf_op jit(solution)/shard_map/while/body/eval_jaxpr/div | solution.py:186
  258.5 19.9 %fusion.565 = (f32[128]{0:T(128)S(1)}, f32[128]{0:T(128)S(1)}, f32[128]{0:T(128)S(1)}, f32[128]{0:T(128)S(1)}, f32[128]{0:T(128)S(1)}, /*index=5*/f32[128]{0:T(1...) fusion(f32[3,32,128]{2,1,0:T(8,128)S(1)} %get-tuple-element.125, ...), kind=kLoop, calls=%fused_computation.41.clone.1 | loop fusion | flops 12288 | bytes 33664 | tf_op jit(solution)/shard_map/while/body/eval_jaxpr/div | solution.py:186
  341.0 19.5 %fusion.330 = (f32[128]{0:T(128)S(1)}, f32[128]{0:T(128)S(1)}, f32[128]{0:T(128)S(1)}, f32[128]{0:T(128)S(1)}, f32[128]{0:T(128)S(1)}, /*index=5*/f32[128]{0:T(1...) fusion(f32[128,128]{1,0:T(8,128)S(1)} %fusion.256, ...), kind=kLoop, calls=%fused_computation.656 | loop fusion | flops 11904 | bytes 32504 | tf_op jit(solution)/shard_map/eval_jaxpr/div | solution.py:186
  360.9 66.0 %while.33 = (s32[]{:T(128)}, f32[128]{0:T(128)S(1)}, f32[3,32,128]{2,1,0:T(8,128)S(1)}, f32[3,32,128]{2,1,0:T(8,128)S(1)}, f32[3,32]{1,0:T(4,128)S(1)}, /*index=...) while((s32[]{:T(128)}, f32[128]{0:T(128)S(1)}, ...), condition=%wide.region_3.4_spmd, body=%wide.region_2.3_spmd.sunk | while | flops 8226 | bytes 101341 | solution.py:186
  362.3 20.4 %fusion.568 = (f32[128]{0:T(128)S(1)}, f32[128]{0:T(128)S(1)}, f32[128]{0:T(128)S(1)}, f32[128]{0:T(128)S(1)}, f32[128]{0:T(128)S(1)}, /*index=5*/f32[128]{0:T(1...) fusion(f32[3,32,128]{2,1,0:T(8,128)S(1)} %get-tuple-element.136, ...), kind=kLoop, calls=%fused_computation.169.clone.1 | loop fusion | flops 8192 | bytes 33536 | tf_op jit(solution)/shard_map/while/body/eval_jaxpr/sub | solution.py:186
  384.3 20.4 %fusion.568 = (f32[128]{0:T(128)S(1)}, f32[128]{0:T(128)S(1)}, f32[128]{0:T(128)S(1)}, f32[128]{0:T(128)S(1)}, f32[128]{0:T(128)S(1)}, /*index=5*/f32[128]{0:T(1...) fusion(f32[3,32,128]{2,1,0:T(8,128)S(1)} %get-tuple-element.136, ...), kind=kLoop, calls=%fused_computation.169.clone.1 | loop fusion | flops 8192 | bytes 33536 | tf_op jit(solution)/shard_map/while/body/eval_jaxpr/sub | solution.py:186
  406.4 20.4 %fusion.568 = (f32[128]{0:T(128)S(1)}, f32[128]{0:T(128)S(1)}, f32[128]{0:T(128)S(1)}, f32[128]{0:T(128)S(1)}, f32[128]{0:T(128)S(1)}, /*index=5*/f32[128]{0:T(1...) fusion(f32[3,32,128]{2,1,0:T(8,128)S(1)} %get-tuple-element.136, ...), kind=kLoop, calls=%fused_computation.169.clone.1 | loop fusion | flops 8192 | bytes 33536 | tf_op jit(solution)/shard_map/while/body/eval_jaxpr/sub | solution.py:186
  576.0 15.8 %fusion.181 = f32[128,16,256]{2,1,0:T(8,128)S(1)} fusion(bf16[128,16,256]{2,1,0:T(8,128)(2,1)S(1)} %copy-done, bf16[128,16,256]{2,1,0:T(8,128)(2,1)S(1)} %copy-done.1, f32[128,16,256]{2,1,0:T(8,128)} %param.14, f32[1,16,256]{2,1,0:T(8,128)} %collective-permute-done.1, f32[1,16,256]{2,1,0:T(8,128)S(1)} %collective-permute-done, ...), kind=kLoop, calls=%fused_computation.299 | loop fusion | flops 28311552 | bytes 10816000 | tf_op jit(solution)/shard_map/add | solution.py:86
  609.2 13.6 %subtract_divide_fusion.5 = (f32[1,4096]{1,0:T(1,128)S(1)}, f32[1,4096]{1,0:T(1,128)S(1)}) fusion(f32[]{:T(128)} %bitcast.672, f32[]{:T(128)S(6)} %sub.2797, f32[]{:T(128)S(1)} %bitcast.2392, f32[128,4096]{1,0:T(8,128)S(1)} %fusion.531, f32[]{:T(128)S(6)} %sub.2802, f32[]{:T(128)} %bitcast.670, f32[]{:T(128)} %bitcast.640, f32[]{:T(128)} %bitcast.639, ...), kind=kLoop, calls=%fused_computation.547 | loop fusion | flops 286720 | bytes 196748 | tf_op jit(solution)/shard_map/div | solution.py:143
  653.7 9.4 fusion.185
  678.7 13.6 %subtract_divide_fusion.4 = (f32[1,4096]{1,0:T(1,128)S(1)}, f32[1,4096]{1,0:T(1,128)S(1)}) fusion(f32[]{:T(128)} %bitcast.672, f32[]{:T(128)S(6)} %sub.2797, f32[]{:T(128)S(1)} %bitcast.2393, f32[128,4096]{1,0:T(8,128)S(1)} %fusion.532, f32[]{:T(128)S(6)} %sub.2802, f32[]{:T(128)} %bitcast.670, f32[]{:T(128)} %bitcast.640, f32[]{:T(128)} %bitcast.639, ...), kind=kLoop, calls=%fused_computation.546 | loop fusion | flops 286720 | bytes 196748 | tf_op jit(solution)/shard_map/div | solution.py:143
  723.3 9.4 fusion.189
  737.0 6.2 all-to-all-start.2
  748.5 13.6 %subtract_divide_fusion.3 = (f32[1,4096]{1,0:T(1,128)S(1)}, f32[1,4096]{1,0:T(1,128)S(1)}) fusion(f32[]{:T(128)} %bitcast.672, f32[]{:T(128)S(6)} %sub.2797, f32[]{:T(128)S(1)} %bitcast.2394, f32[128,4096]{1,0:T(8,128)S(1)} %fusion.533, f32[]{:T(128)S(6)} %sub.2802, f32[]{:T(128)} %bitcast.670, f32[]{:T(128)} %bitcast.640, f32[]{:T(128)} %bitcast.639, ...), kind=kLoop, calls=%fused_computation.545 | loop fusion | flops 286720 | bytes 196748 | tf_op jit(solution)/shard_map/div | solution.py:143
  793.4 9.4 fusion.193
  807.0 6.2 all-to-all-start.3
  818.6 13.6 %subtract_divide_fusion.2 = (f32[1,4096]{1,0:T(1,128)S(1)}, f32[1,4096]{1,0:T(1,128)S(1)}) fusion(f32[]{:T(128)} %bitcast.672, f32[]{:T(128)S(6)} %sub.2797, f32[]{:T(128)S(1)} %bitcast.2395, f32[128,4096]{1,0:T(8,128)S(1)} %fusion.534, f32[]{:T(128)S(6)} %sub.2802, f32[]{:T(128)} %bitcast.670, f32[]{:T(128)} %bitcast.640, f32[]{:T(128)} %bitcast.639, ...), kind=kLoop, calls=%fused_computation.544 | loop fusion | flops 286720 | bytes 196748 | tf_op jit(solution)/shard_map/div | solution.py:143
  863.1 9.4 fusion.197
  888.3 13.6 %subtract_divide_fusion.1 = (f32[1,4096]{1,0:T(1,128)S(1)}, f32[1,4096]{1,0:T(1,128)S(1)}) fusion(f32[]{:T(128)} %bitcast.672, f32[]{:T(128)S(6)} %sub.2797, f32[]{:T(128)S(1)} %bitcast.2396, f32[128,4096]{1,0:T(8,128)S(1)} %fusion.535, f32[]{:T(128)S(6)} %sub.2802, f32[]{:T(128)} %bitcast.670, f32[]{:T(128)} %bitcast.640, f32[]{:T(128)} %bitcast.639, ...), kind=kLoop, calls=%fused_computation.543 | loop fusion | flops 286720 | bytes 196748 | tf_op jit(solution)/shard_map/div | solution.py:143
  932.9 9.4 fusion.201
  946.6 6.2 all-to-all-start.5
  958.1 13.6 %subtract_divide_fusion = (f32[1,4096]{1,0:T(1,128)S(1)}, f32[1,4096]{1,0:T(1,128)S(1)}) fusion(f32[]{:T(128)} %bitcast.672, f32[]{:T(128)S(6)} %sub.2797, f32[]{:T(128)S(1)} %bitcast.2397, f32[128,4096]{1,0:T(8,128)S(1)} %fusion.536, f32[]{:T(128)S(6)} %sub.2802, f32[]{:T(128)} %bitcast.670, f32[]{:T(128)} %bitcast.640, f32[]{:T(128)} %bitcast.639, ...), kind=kLoop, calls=%fused_computation.542 | loop fusion | flops 286720 | bytes 196748 | tf_op jit(solution)/shard_map/div | solution.py:143
  (369 shorter events, 365.6 us)
Async XLA Ops:
  1.4 574.6 %collective-permute-start.1 = (f32[1,16,256]{2,1,0:T(8,128)}, f32[1,16,256]{2,1,0:T(8,128)}, u32[]{:S(2)}, u32[]{:S(2)}) collective-permute-start(f32[1,16,256]{2,1,0:T(8,128)} %get-tuple-element.511), channel_id=1, source_target_pairs={{0,1},{1,2},{2,3},{4,5},{5,6},{6,7},{8,9},{9,10},{10,11},{12,13},{... | collective-permute-start | bytes 49160 | tf_op jit(solution)/shard_map/ppermute | solution.py:21
  6.8 569.1 %collective-permute-start.5 = (f32[128,2,256]{2,1,0:T(2,128)}, f32[128,2,256]{2,1,0:T(2,128)S(1)}, u32[]{:S(2)}, u32[]{:S(2)}) collective-permute-start(f32[128,2,256]{2,1,0:T(2,128)} %get-tuple-element.509), channel_id=1, source_target_pairs={{0,4},{4,8},{8,12},{12,0},{1,5},{5,9},{9,13},{13,1},{2,6},{6,10},{... | collective-permute-start | bytes 786440 | tf_op jit(solution)/shard_map/ppermute | solution.py:21
  9.2 565.0 %collective-permute-start.4 = (f32[128,2,256]{2,1,0:T(2,128)}, f32[128,2,256]{2,1,0:T(2,128)}, u32[]{:S(2)}, u32[]{:S(2)}) collective-permute-start(f32[128,2,256]{2,1,0:T(2,128)} %get-tuple-element.508), channel_id=1, source_target_pairs={{4,0},{8,4},{12,8},{0,12},{5,1},{9,5},{13,9},{1,13},{6,2},{10,6},{... | collective-permute-start | bytes 786440 | tf_op jit(solution)/shard_map/ppermute | solution.py:24
  14.2 554.8 %collective-permute-start.2 = (f32[128,16,2]{0,1,2:T(8,128)}, f32[128,16,2]{0,1,2:T(8,128)}, u32[]{:S(2)}, u32[]{:S(2)}) collective-permute-start(f32[128,16,2]{0,1,2:T(8,128)} %copy.101), channel_id=1, source_target_pairs={{16,0},{17,1},{18,2},{19,3},{20,4},{21,5},{22,6},{23,7},{24,8},{25... | collective-permute-start | bytes 49160 | tf_op jit(solution)/shard_map/ppermute | solution.py:24
  16.5 555.5 %collective-permute-start.3 = (f32[128,16,2]{0,1,2:T(8,128)}, f32[128,16,2]{0,1,2:T(8,128)}, u32[]{:S(2)}, u32[]{:S(2)}) collective-permute-start(f32[128,16,2]{0,1,2:T(8,128)} %copy.102), channel_id=1, source_target_pairs={{0,16},{1,17},{2,18},{3,19},{4,20},{5,21},{6,22},{7,23},{8,24},{9,... | collective-permute-start | bytes 49160 | tf_op jit(solution)/shard_map/ppermute | solution.py:21
  596.1 13.1 %all-to-all-start = ((f32[4,1,4096]{2,1,0:T(1,128)}), f32[4,1,4096]{2,1,0:T(1,128)S(1)}, u32[]{:S(2)}, u32[]{:S(2)}) async-start(f32[4,1,4096]{2,1,0:T(1,128)} %stack.741), calls=%async_computation | async-start | bytes 131072 | tf_op jit(solution)/shard_map/all_to_all | solution.py:159
  627.2 26.6 %collective-permute-start.11 = (f32[128,2,256]{2,1,0:T(2,128)}, f32[128,2,256]{2,1,0:T(2,128)S(1)}, u32[]{:S(2)}, u32[]{:S(2)}) collective-permute-start(f32[128,2,256]{2,1,0:T(2,128)} %get-tuple-element.503), channel_id=1, source_target_pairs={{0,4},{4,8},{8,12},{12,0},{1,5},{5,9},{9,13},{13,1},{2,6},{6,10},{... | collective-permute-start | bytes 786440 | tf_op jit(solution)/shard_map/ppermute | solution.py:21
  627.2 24.8 %collective-permute-start.10 = (f32[128,2,256]{2,1,0:T(2,128)}, f32[128,2,256]{2,1,0:T(2,128)}, u32[]{:S(2)}, u32[]{:S(2)}) collective-permute-start(f32[128,2,256]{2,1,0:T(2,128)} %get-tuple-element.502), channel_id=1, source_target_pairs={{4,0},{8,4},{12,8},{0,12},{5,1},{9,5},{13,9},{1,13},{6,2},{10,6},{... | collective-permute-start | bytes 786440 | tf_op jit(solution)/shard_map/ppermute | solution.py:24
  634.7 12.2 %collective-permute-start.8 = (f32[128,16,2]{0,1,2:T(8,128)}, f32[128,16,2]{0,1,2:T(8,128)S(1)}, u32[]{:S(2)}, u32[]{:S(2)}) collective-permute-start(f32[128,16,2]{0,1,2:T(8,128)} %copy.103), channel_id=1, source_target_pairs={{16,0},{17,1},{18,2},{19,3},{20,4},{21,5},{22,6},{23,7},{24,8},{25... | collective-permute-start | bytes 49160 | tf_op jit(solution)/shard_map/ppermute | solution.py:24
  696.7 26.6 %collective-permute-start.17 = (f32[128,2,256]{2,1,0:T(2,128)}, f32[128,2,256]{2,1,0:T(2,128)S(1)}, u32[]{:S(2)}, u32[]{:S(2)}) collective-permute-start(f32[128,2,256]{2,1,0:T(2,128)} %get-tuple-element.497), channel_id=1, source_target_pairs={{0,4},{4,8},{8,12},{12,0},{1,5},{5,9},{9,13},{13,1},{2,6},{6,10},{... | collective-permute-start | bytes 786440 | tf_op jit(solution)/shard_map/ppermute | solution.py:21
  696.7 24.8 %collective-permute-start.16 = (f32[128,2,256]{2,1,0:T(2,128)}, f32[128,2,256]{2,1,0:T(2,128)}, u32[]{:S(2)}, u32[]{:S(2)}) collective-permute-start(f32[128,2,256]{2,1,0:T(2,128)} %get-tuple-element.496), channel_id=1, source_target_pairs={{4,0},{8,4},{12,8},{0,12},{5,1},{9,5},{13,9},{1,13},{6,2},{10,6},{... | collective-permute-start | bytes 786440 | tf_op jit(solution)/shard_map/ppermute | solution.py:24
  704.3 12.2 %collective-permute-start.14 = (f32[128,16,2]{0,1,2:T(8,128)}, f32[128,16,2]{0,1,2:T(8,128)S(1)}, u32[]{:S(2)}, u32[]{:S(2)}) collective-permute-start(f32[128,16,2]{0,1,2:T(8,128)} %copy.105), channel_id=1, source_target_pairs={{16,0},{17,1},{18,2},{19,3},{20,4},{21,5},{22,6},{23,7},{24,8},{25... | collective-permute-start | bytes 49160 | tf_op jit(solution)/shard_map/ppermute | solution.py:24
  707.8 11.6 %collective-permute-start.15 = (f32[128,16,2]{0,1,2:T(8,128)}, f32[128,16,2]{0,1,2:T(8,128)}, u32[]{:S(2)}, u32[]{:S(2)}) collective-permute-start(f32[128,16,2]{0,1,2:T(8,128)} %copy.106), channel_id=1, source_target_pairs={{0,16},{1,17},{2,18},{3,19},{4,20},{5,21},{6,22},{7,23},{8,24},{9,... | collective-permute-start | bytes 49160 | tf_op jit(solution)/shard_map/ppermute | solution.py:21
  766.5 26.8 %collective-permute-start.23 = (f32[128,2,256]{2,1,0:T(2,128)}, f32[128,2,256]{2,1,0:T(2,128)S(1)}, u32[]{:S(2)}, u32[]{:S(2)}) collective-permute-start(f32[128,2,256]{2,1,0:T(2,128)} %get-tuple-element.491), channel_id=1, source_target_pairs={{0,4},{4,8},{8,12},{12,0},{1,5},{5,9},{9,13},{13,1},{2,6},{6,10},{... | collective-permute-start | bytes 786440 | tf_op jit(solution)/shard_map/ppermute | solution.py:21
  766.5 25.0 %collective-permute-start.22 = (f32[128,2,256]{2,1,0:T(2,128)}, f32[128,2,256]{2,1,0:T(2,128)}, u32[]{:S(2)}, u32[]{:S(2)}) collective-permute-start(f32[128,2,256]{2,1,0:T(2,128)} %get-tuple-element.490), channel_id=1, source_target_pairs={{4,0},{8,4},{12,8},{0,12},{5,1},{9,5},{13,9},{1,13},{6,2},{10,6},{... | collective-permute-start | bytes 786440 | tf_op jit(solution)/shard_map/ppermute | solution.py:24
  774.1 12.2 %collective-permute-start.20 = (f32[128,16,2]{0,1,2:T(8,128)}, f32[128,16,2]{0,1,2:T(8,128)S(1)}, u32[]{:S(2)}, u32[]{:S(2)}) collective-permute-start(f32[128,16,2]{0,1,2:T(8,128)} %copy.107), channel_id=1, source_target_pairs={{16,0},{17,1},{18,2},{19,3},{20,4},{21,5},{22,6},{23,7},{24,8},{25... | collective-permute-start | bytes 49160 | tf_op jit(solution)/shard_map/ppermute | solution.py:24
  777.6 11.8 %collective-permute-start.21 = (f32[128,16,2]{0,1,2:T(8,128)}, f32[128,16,2]{0,1,2:T(8,128)}, u32[]{:S(2)}, u32[]{:S(2)}) collective-permute-start(f32[128,16,2]{0,1,2:T(8,128)} %copy.108), channel_id=1, source_target_pairs={{0,16},{1,17},{2,18},{3,19},{4,20},{5,21},{6,22},{7,23},{8,24},{9,... | collective-permute-start | bytes 49160 | tf_op jit(solution)/shard_map/ppermute | solution.py:21
  836.5 26.6 %collective-permute-start.29 = (f32[128,2,256]{2,1,0:T(2,128)}, f32[128,2,256]{2,1,0:T(2,128)S(1)}, u32[]{:S(2)}, u32[]{:S(2)}) collective-permute-start(f32[128,2,256]{2,1,0:T(2,128)} %get-tuple-element.485), channel_id=1, source_target_pairs={{0,4},{4,8},{8,12},{12,0},{1,5},{5,9},{9,13},{13,1},{2,6},{6,10},{... | collective-permute-start | bytes 786440 | tf_op jit(solution)/shard_map/ppermute | solution.py:21
  836.5 24.8 %collective-permute-start.28 = (f32[128,2,256]{2,1,0:T(2,128)}, f32[128,2,256]{2,1,0:T(2,128)}, u32[]{:S(2)}, u32[]{:S(2)}) collective-permute-start(f32[128,2,256]{2,1,0:T(2,128)} %get-tuple-element.484), channel_id=1, source_target_pairs={{4,0},{8,4},{12,8},{0,12},{5,1},{9,5},{13,9},{1,13},{6,2},{10,6},{... | collective-permute-start | bytes 786440 | tf_op jit(solution)/shard_map/ppermute | solution.py:24
  844.1 12.2 %collective-permute-start.26 = (f32[128,16,2]{0,1,2:T(8,128)}, f32[128,16,2]{0,1,2:T(8,128)S(1)}, u32[]{:S(2)}, u32[]{:S(2)}) collective-permute-start(f32[128,16,2]{0,1,2:T(8,128)} %copy.109), channel_id=1, source_target_pairs={{16,0},{17,1},{18,2},{19,3},{20,4},{21,5},{22,6},{23,7},{24,8},{25... | collective-permute-start | bytes 49160 | tf_op jit(solution)/shard_map/ppermute | solution.py:24
  906.3 26.6 %collective-permute-start.35 = (f32[128,2,256]{2,1,0:T(2,128)}, f32[128,2,256]{2,1,0:T(2,128)S(1)}, u32[]{:S(2)}, u32[]{:S(2)}) collective-permute-start(f32[128,2,256]{2,1,0:T(2,128)} %get-tuple-element.479), channel_id=1, source_target_pairs={{0,4},{4,8},{8,12},{12,0},{1,5},{5,9},{9,13},{13,1},{2,6},{6,10},{... | collective-permute-start | bytes 786440 | tf_op jit(solution)/shard_map/ppermute | solution.py:21
  906.3 24.8 %collective-permute-start.34 = (f32[128,2,256]{2,1,0:T(2,128)}, f32[128,2,256]{2,1,0:T(2,128)}, u32[]{:S(2)}, u32[]{:S(2)}) collective-permute-start(f32[128,2,256]{2,1,0:T(2,128)} %get-tuple-element.478), channel_id=1, source_target_pairs={{4,0},{8,4},{12,8},{0,12},{5,1},{9,5},{13,9},{1,13},{6,2},{10,6},{... | collective-permute-start | bytes 786440 | tf_op jit(solution)/shard_map/ppermute | solution.py:24
  913.9 12.2 %collective-permute-start.32 = (f32[128,16,2]{0,1,2:T(8,128)}, f32[128,16,2]{0,1,2:T(8,128)S(1)}, u32[]{:S(2)}, u32[]{:S(2)}) collective-permute-start(f32[128,16,2]{0,1,2:T(8,128)} %copy.111), channel_id=1, source_target_pairs={{16,0},{17,1},{18,2},{19,3},{20,4},{21,5},{22,6},{23,7},{24,8},{25... | collective-permute-start | bytes 49160 | tf_op jit(solution)/shard_map/ppermute | solution.py:24
  917.4 11.6 %collective-permute-start.33 = (f32[128,16,2]{0,1,2:T(8,128)}, f32[128,16,2]{0,1,2:T(8,128)}, u32[]{:S(2)}, u32[]{:S(2)}) collective-permute-start(f32[128,16,2]{0,1,2:T(8,128)} %copy.112), channel_id=1, source_target_pairs={{0,16},{1,17},{2,18},{3,19},{4,20},{5,21},{6,22},{7,23},{8,24},{9,... | collective-permute-start | bytes 49160 | tf_op jit(solution)/shard_map/ppermute | solution.py:21
  (29 other events, 459.2 us)
